TPU v7x, 32 devices: a whole 2x2x4 slice. The times are simulated.
32 devices in a mesh: groups: 2 (over x), tile: 16 (over z, y, core).
Axes of the slice: x: 2, y: 2, z: 4, core: 2. Of those that a mesh axis runs over, the one named last changes fastest.
Arguments:
- data_halves: bfloat16 [2, 4, 256, 32, 512], P(None, None, ('groups', 'tile')), parts along dimension 2, may hold values from 0.1 to 20, as said below
- psf_taps: float32 [4, 3, 9], replicated, may hold values from 0.05 to 1
- cycle_map: int32 [32, 32, 512], P(('groups', 'tile')), parts along dimension 0, may hold values from 0 to 255, as said below
- cutoff: int32 [2], P('groups'), parts along dimension 0, may hold values from 64 to 255
Outputs:
- joined: float32 [256, 32, 512], P(('groups', 'tile')), parts along dimension 0
There are 2 independent parts, one for each index of `groups`. A program takes and returns all parts, laid end to end along the dimension named above; an argument that names none is the same for every part. Nothing has to cross between parts.
Inputs may be any that keep to these rules, and one draw needn't show every extreme that they name: `data_halves`: positive photon counts. cycle_map[b, k, l] is the cycle of frequency (k, l) in block b: with fk = min(k, 32 - k), fl = min(l, 512 - l) and a whole stretch s_b of 1 to 4 drawn for each block, the largest r with r * r <= (s_b fk)^2 + fl^2, capped at 255.
All inputs are finite; a program needn't handle non-finite values.
Results may differ from a plain program's by a relative error of at most 0.00095.
The roundings to bfloat16 on the way count: a program that leaves them out, or rounds other values in their place, can miss the bound.
Values may be sent and summed in bfloat16 or wider, within the bound.
A program may use at most 64 MiB of HBM per device.

v0:
```python
import functools

import jax
import jax.numpy as jnp
import ml_dtypes
import numpy as np
from jax import lax
from jax.experimental import pallas as pl
from jax.experimental.pallas import tpu as pltpu
from jax.sharding import PartitionSpec as P

ITERS = 2
CYCLES = 256
MESH = pl.DeviceIdType.MESH
F32 = jnp.float32
BF16 = jnp.bfloat16


def cos_sin(length):
    index_n = np.arange(length)
    phase = index_n[:, None] * index_n[None, :] % length
    angle = phase.astype(np.float32) * np.float32(2.0 * np.pi / length)
    return np.cos(angle).astype(np.float32), np.sin(angle).astype(np.float32)


def split_np(matrix):
    high = matrix.astype(ml_dtypes.bfloat16)
    low = (matrix - high.astype(np.float32)).astype(ml_dtypes.bfloat16)
    return np.concatenate([high, low, high], axis=1)


def constants(depth, lateral):
    half = depth // 2
    order = np.concatenate([np.arange(half + 1), depth - np.arange(1, half)])
    cos_z, sin_z = cos_sin(depth)
    cos_z, sin_z = cos_z[order], sin_z[order]
    eye = np.eye(128 // depth, dtype=np.float32)
    cos_k, sin_k = np.kron(eye, cos_z), np.kron(eye, sin_z)
    forward = np.block([[cos_k, sin_k], [-sin_k, cos_k]])
    inverse = np.ascontiguousarray(forward.T)
    cos_y, sin_y = cos_sin(lateral)
    lateral_table = np.concatenate([cos_y, -sin_y], axis=1).astype(ml_dtypes.bfloat16)
    return lateral_table, split_np(forward), split_np(inverse)


def split(value):
    high = value.astype(BF16)
    low = (value - high.astype(F32)).astype(BF16)
    return high, low


def dot(a, b):
    return lax.dot_general(a, b, (((1,), (0,)), ((), ())), preferred_element_type=F32)


def kernel(
    n, data, psf, cycles, cutoff, table, forward_z, inverse_z, out,
    est, halo, corr_out, corr_in, corr_own, spread, gather, lat_f, lat_b,
    dext, first, cs, onehot, spec, folded, red_out, red_in,
    halo_send, halo_recv, corr_send, corr_recv, red_send, red_recv,
):
    me = lax.axis_index("tile")
    has_left = me > 0
    has_right = me < n - 1

    barrier = pltpu.get_barrier_semaphore()

    def greet(step, carry):
        peer = lax.rem(me + step, n)
        pl.semaphore_signal(barrier, inc=1, device_id={"tile": peer}, device_id_type=MESH)
        return carry

    lax.fori_loop(1, n, greet, 0)

    for h in range(2):
        total = data[h, 0].astype(F32)
        for v in range(1, 4):
            total = total + data[h, v].astype(F32)
        est[h] = total * 0.25

    pl.semaphore_wait(barrier, n - 1)

    def halo_copy(it, h, side):
        peer = lax.rem(me + n - 1, n) if side == 0 else lax.rem(me + 1, n)
        return pltpu.make_async_remote_copy(
            src_ref=est.at[h, pl.ds(128 * side, 128)],
            dst_ref=halo.at[it, h, 1 - side],
            send_sem=halo_send.at[it, h, side],
            recv_sem=halo_recv.at[it, h, 1 - side],
            device_id={"tile": peer},
            device_id_type=MESH,
        )

    def corr_copy(it, h, side):
        peer = lax.rem(me + n - 1, n) if side == 0 else lax.rem(me + 1, n)
        return pltpu.make_async_remote_copy(
            src_ref=corr_out.at[it, h, side],
            dst_ref=corr_in.at[it, h, 1 - side],
            send_sem=corr_send.at[it, h, side],
            recv_sem=corr_recv.at[it, h, 1 - side],
            device_id={"tile": peer},
            device_id_type=MESH,
        )

    def on_side(side, action):
        pl.when(has_left if side == 0 else has_right)(action)

    def start(make, it, h):
        for side in range(2):
            on_side(side, lambda: make(it, h, side).start())

    def wait_recv(make, it, h):
        for side in range(2):
            on_side(side, lambda: make(it, h, 1 - side).wait_recv())

    def wait_send(make, it, h):
        for side in range(2):
            on_side(side, lambda: make(it, h, side).wait_send())

    start(halo_copy, 0, 0)
    start(halo_copy, 0, 1)

    def clear(side):
        for it in range(ITERS):
            for h in range(2):
                halo[it, h, side] = jnp.zeros((128, halo.shape[-1]), F32)
                corr_in[it, h, side] = jnp.zeros((128, halo.shape[-1]), F32)

    pl.when(jnp.logical_not(has_left))(lambda: clear(0))
    pl.when(jnp.logical_not(has_right))(lambda: clear(1))

    row = lax.broadcasted_iota(jnp.int32, (128, 128), 0)
    col = lax.broadcasted_iota(jnp.int32, (128, 128), 1)
    depth = data.shape[2] // 8
    shift_y = row - col + 4
    shift_z = col % depth - row % depth + 4
    shift_x = col // depth - row // depth

    def taps_of(v, axis):
        taps = [psf[v, axis, t] for t in range(9)]
        total = taps[0]
        for t in range(1, 9):
            total = total + taps[t]
        return taps, jnp.ones((128, 128), F32) / jnp.full((128, 128), total, F32)

    def select(shift, taps, low, high):
        value = jnp.zeros((128, 128), F32)
        for t in range(low, high):
            value = jnp.where(shift == t, taps[t], value)
        return value

    zero = jnp.zeros((128, 128), BF16)

    def build(v, carry):
        for mirrored in range(2):
            (kx, nx), (ky, ny), (kz, nz) = taps_of(v, 0), taps_of(v, 2), taps_of(v, 1)
            if mirrored:
                kx, ky, kz = kx[::-1], ky[::-1], kz[::-1]
            band_z = select(shift_z, kz, 0, 9) * (nx * nz)
            at_v = pl.ds(pl.multiple_of(v * 128, 128), 128)
            for s in range(3):
                low, high = split(select(shift_x + 4 * s, kx, max(4 * s - 3, 0), min(4 * s + 4, 9)) * band_z)
                for part, value in enumerate((low, high, low)):
                    if mirrored:
                        column = pl.ds(pl.multiple_of(v * 384 + part * 128, 128), 128)
                        gather[pl.ds(256 - 128 * s, 128), column] = value
                    else:
                        spread[at_v, pl.ds(384 * s + 128 * part, 128)] = value
            lat = lat_b if mirrored else lat_f
            same = split(select(shift_y, ky, 0, 9) * ny)
            after = split(select(shift_y + 128, ky, 0, 4 + 5) * ny)
            before = split(select(shift_y - 128, ky, 0, 9) * ny)
            for part, which in enumerate((0, 1, 0)):
                for b in range(2):
                    for i in range(3):
                        for o in range(2):
                            step = (i + b) - (o + 2 * b)
                            value = {0: same, 1: after, -1: before}.get(step)
                            value = zero if value is None else value[which]
                            lat[v, b, pl.ds(384 * part + 128 * i, 128), pl.ds(128 * o, 128)] = value
        return carry

    lax.fori_loop(0, 4, build, 0)

    bins = lax.broadcasted_iota(jnp.int32, (CYCLES, 256), 0)

    def mark(k, carry):
        ids = cycles[0, pl.ds(k, 1), pl.ds(0, 256)]
        onehot[k] = jnp.where(bins == ids, 1.0, 0.0).astype(BF16)
        return carry

    lax.fori_loop(0, depth // 2 + 1, mark, 0)

    def put_parts(ref, base, value):
        high, low = split(value)
        ref[pl.ds(base, 128)] = high
        ref[pl.ds(base + 128, 128)] = high
        ref[pl.ds(base + 256, 128)] = low

    def along_y(value, lat, v):
        high, low = split(value)
        for b in range(2):
            at = slice(128 * b, 128 * b + 384)
            lhs = jnp.concatenate([high[:, at], high[:, at], low[:, at]], axis=1)
            yield dot(lhs, lat[v, b])

    def sweep(it, h):
        put_parts(dext, 0, halo[it, h, 0])
        put_parts(dext, 384, est[h, pl.ds(0, 128)])
        put_parts(dext, 768, est[h, pl.ds(128, 128)])
        put_parts(dext, 1152, halo[it, h, 1])
        for i in range(2):
            first[i] = dot(spread[...], dext[pl.ds(384 * i, 1152)])

        def view(v, carry):
            at_v = pl.ds(pl.multiple_of(v * 128, 128), 128)
            value = jnp.concatenate([first[0, at_v], first[1, at_v]], axis=0)
            quotient = [
                data[h, v, :, pl.ds(256 * b, 256)].astype(F32) / predicted
                for b, predicted in enumerate(along_y(value, lat_f, v))
            ]
            quotient = jnp.concatenate(quotient, axis=1)
            for b, corrected in enumerate(along_y(quotient, lat_b, v)):
                high, low = split(corrected)
                for part, piece in enumerate((high, high, low)):
                    at = pl.ds(pl.multiple_of(v * 384 + 128 * part, 128), 128)
                    for side in range(2):
                        cs[side, at, pl.ds(256 * b, 256)] = piece[128 * side : 128 * side + 128]
            return carry

        lax.fori_loop(0, 4, view, 0)
        r0 = dot(gather[...], cs[0])
        corr_out[it, h, 0] = r0[:128]
        corr_own[h] = r0[128:]
        r1 = dot(gather[...], cs[1])
        corr_out[it, h, 1] = r1[256:]
        corr_own[h] += r1[:256]

    def update(it, h):
        wait_send(halo_copy, it, h)
        wait_recv(corr_copy, it, h)
        for side in range(2):
            at = pl.ds(128 * side, 128)
            est[h, at] = est[h, at] * (0.25 * (corr_own[h, at] + corr_in[it, h, side]))

    def spectrum(h):
        rows = dot(est[h].astype(BF16), table[...])
        lateral = rows.shape[1] // 2
        for g in range(2):
            at = slice(128 * g, 128 * g + 128)
            both = jnp.concatenate([rows[at, :lateral], rows[at, lateral:]], axis=0)
            high, low = split(both)
            spec[h, g] = dot(forward_z[...], jnp.concatenate([high, high, low], axis=0))

    for it in range(ITERS):
        for h in range(2):
            wait_recv(halo_copy, it, h)
            sweep(it, h)
            start(corr_copy, it, h)
        for h in range(2):
            update(it, h)
            if it + 1 < ITERS:
                start(halo_copy, it + 1, h)
            else:
                spectrum(h)

    lateral = data.shape[3]
    half = depth // 2

    def power(a, b):
        total = jnp.zeros((depth, lateral), F32)
        for g in range(2):
            for at in range(0, 256, depth):
                total = total + spec[a, g, pl.ds(at, depth)] * spec[b, g, pl.ds(at, depth)]
        return total

    lane = lax.broadcasted_iota(jnp.int32, (1, 256), 1)
    weight_l = jnp.where(lane == 0, 1.0, 2.0)
    rows16 = lax.broadcasted_iota(jnp.int32, (half, 256), 0)
    folded[...] = jnp.zeros_like(folded)
    edge = []
    for q, (a, b) in enumerate(((0, 1), (0, 0), (1, 1))):
        total = power(a, b)
        edge.append(jnp.sum(total[:, 256:257], axis=0, keepdims=True))
        low = total[:half, :256]
        high = total[half:, :256]
        pairs = (low + jnp.where(rows16 == 0, 0.0, high)) * weight_l
        last = high[:1] * weight_l
        for k in range(half):
            folded[k, q : q + 1] = pairs[k : k + 1]
        folded[half, q : q + 1] = last

    binned = jnp.zeros((32, CYCLES), F32)
    for k in range(half + 1):
        value = folded[k]
        a = value.astype(BF16).astype(F32)
        b = (value - a).astype(BF16).astype(F32)
        c = value - a - b
        lhs = jnp.concatenate([a, b, c, jnp.zeros_like(a)], axis=0).astype(BF16)
        binned = binned + lax.dot_general(
            lhs, onehot[k], (((1,), (1,)), ((), ())), preferred_element_type=F32
        )
    binned = binned[0:8] + binned[8:16] + binned[16:24]
    bin_row = lax.broadcasted_iota(jnp.int32, (8, CYCLES), 0)
    bin_lane = lax.broadcasted_iota(jnp.int32, (8, CYCLES), 1)
    for q in range(3):
        binned = binned + jnp.where(
            (bin_row == q) & (bin_lane == CYCLES - 1), jnp.broadcast_to(edge[q], (8, CYCLES)), 0.0
        )
    red_out[...] = binned

    def share(step):
        peer = lax.rem(me + step, n)
        return pltpu.make_async_remote_copy(
            src_ref=red_out,
            dst_ref=red_in.at[step],
            send_sem=red_send.at[step],
            recv_sem=red_recv.at[step],
            device_id={"tile": peer},
            device_id_type=MESH,
        )

    def start_share(step, carry):
        share(step).start()
        return carry

    def wait_share(step, carry):
        share(step).wait()
        return carry + red_in[step]

    lax.fori_loop(1, n, start_share, 0)
    totals = lax.fori_loop(1, n, wait_share, binned)

    corr = totals[0:1] / (jnp.sqrt(totals[1:2]) * jnp.sqrt(totals[2:3]))
    scale = 0.5 / (depth * lateral)
    cycle_weight = jnp.where(lane <= cutoff[0], corr, 0.0) * scale
    low_table = jnp.broadcast_to(cycle_weight[:, :128], (8, 128))
    high_table = jnp.broadcast_to(cycle_weight[:, 128:], (8, 128))
    weights = []
    for r in range(0, half + 8, 8):
        pieces = []
        for c in range(0, lateral, 128):
            ids = cycles[0, pl.ds(r, 8), pl.ds(c, 128)]
            index = ids & 127
            from_low = jnp.take_along_axis(low_table, index, axis=1)
            from_high = jnp.take_along_axis(high_table, index, axis=1)
            pieces.append(jnp.where(ids < 128, from_low, from_high))
        weights.append(jnp.concatenate(pieces, axis=1))
    low = jnp.concatenate(weights[:-1], axis=0)
    row0 = lax.broadcasted_iota(jnp.int32, (half, lateral), 0) == 0
    high = jnp.where(row0, jnp.broadcast_to(weights[-1][0:1], (half, lateral)), low)
    cell = jnp.concatenate([low, high], axis=0)

    for g in range(2):
        mixed = jnp.concatenate(
            [
                (spec[0, g, pl.ds(at, depth)] + spec[1, g, pl.ds(at, depth)]) * cell
                for at in range(0, 256, depth)
            ],
            axis=0,
        )
        high, low = split(mixed)
        inner = dot(inverse_z[...], jnp.concatenate([high, high, low], axis=0)).astype(BF16)
        out[pl.ds(128 * g, 128)] = dot(inner[:128], table[:, pl.ds(0, lateral)]) + dot(
            inner[128:], table[:, pl.ds(lateral, lateral)]
        )

    for it in range(ITERS):
        for h in range(2):
            wait_send(corr_copy, it, h)


def body(data_halves, psf_taps, cycle_map, cutoff):
    halves, views, slab, depth, lateral = data_halves.shape
    n = lax.axis_size("tile")
    rows = slab * depth
    table, forward_z, inverse_z = constants(depth, lateral)
    vmem = pl.BlockSpec(memory_space=pltpu.VMEM)
    smem = pl.BlockSpec(memory_space=pltpu.SMEM)
    dma = pltpu.SemaphoreType.DMA
    joined = pl.pallas_call(
        functools.partial(kernel, n),
        out_shape=jax.ShapeDtypeStruct((rows, lateral), F32),
        in_specs=[vmem, smem, vmem, smem, vmem, vmem, vmem],
        out_specs=vmem,
        scratch_shapes=[
            pltpu.VMEM((2, rows, lateral), F32),
            pltpu.VMEM((ITERS, 2, 2, 128, lateral), F32),
            pltpu.VMEM((ITERS, 2, 2, 128, lateral), F32),
            pltpu.VMEM((ITERS, 2, 2, 128, lateral), F32),
            pltpu.VMEM((2, rows, lateral), F32),
            pltpu.VMEM((512, 1152), BF16),
            pltpu.VMEM((384, 1536), BF16),
            pltpu.VMEM((4, 2, 1152, 256), BF16),
            pltpu.VMEM((4, 2, 1152, 256), BF16),
            pltpu.VMEM((1536, lateral), BF16),
            pltpu.VMEM((2, 512, lateral), F32),
            pltpu.VMEM((2, 1536, lateral), BF16),
            pltpu.VMEM((depth // 2 + 1, CYCLES, 256), BF16),
            pltpu.VMEM((2, 2, rows, lateral), F32),
            pltpu.VMEM((depth // 2 + 1, 8, 256), F32),
            pltpu.VMEM((8, CYCLES), F32),
            pltpu.VMEM((n, 8, CYCLES), F32),
            dma((ITERS, 2, 2)),
            dma((ITERS, 2, 2)),
            dma((ITERS, 2, 2)),
            dma((ITERS, 2, 2)),
            dma((n,)),
            dma((n,)),
        ],
        compiler_params=pltpu.CompilerParams(
            collective_id=0, has_side_effects=True, vmem_limit_bytes=56 * 1024 * 1024
        ),
    )(
        data_halves.reshape(halves, views, rows, lateral),
        psf_taps,
        cycle_map,
        cutoff,
        jnp.asarray(table),
        jnp.asarray(forward_z),
        jnp.asarray(inverse_z),
    )
    return joined.reshape(slab, depth, lateral)


def solution(mesh):
    in_specs = (
        P(None, None, ("groups", "tile"), None, None),
        P(),
        P(("groups", "tile"), None, None),
        P("groups"),
    )
    out_specs = P(("groups", "tile"), None, None)
    return jax.shard_map(body, mesh=mesh, in_specs=in_specs, out_specs=out_specs, check_vma=False)
```

profile of v0, /device:TPU:0, one launch (start us, length us, event | category | flops | bytes accessed | tf_op | source)
XLA Modules:
  0.0 75.6 jit_solution(17241831456007754363)
XLA Ops:
  0.7 1.3 %copy.8.psf = f32[4,3,9]{2,1,0:T(4,128)} copy(f32[4,3,9]{2,0,1:T(4,128)} %param.8) | data formatting | bytes 864 | tf_op args[1]
  1.9 71.7 %shard_map.73 = f32[256,512]{1,0:T(8,128)} custom-call(bf16[2,4,256,512]{3,2,1,0:T(8,128)(2,1)} %bitcast.2, f32[4,3,9]{2,1,0:T(4,128)} %copy.8.psf, s32[1,32,512]{2,1,0:T(8,128)} %cycles.1, s32[1]{0:T(128)S(6)} %copy.10.cutoff, bf16[512,1024]{1,0:T(8,128)(2,1)} %constant.6.clone.table, bf16[256,768]{1,0:T(8,128)(2,1)} %constant.7.clone.forward_z, ...), custom_call_target="tpu_custom_call" | custom-call | tf_op jit(solution)/shard_map/pallas_call | solution.py:381
  73.7 1.9 %copy.11 = f32[8,32,512]{2,1,0:T(8,128)} copy(f32[8,32,512]{2,1,0:T(8,128)} %bitcast.3) | data formatting | bytes 1048576
where the time goes:
time: 75.8 us; the launch traced here: 75.6 us
  Pallas kernels  71.7 us (95%)
  local copies, waits for them, and re-layouts  3.16 us (4%)
    pallas_call x1, Pallas kernels, body(): pl.pallas_call(functools.partial(kernel, n), out_shape=jax.ShapeDtypeStru...  71.7 us
    unnamed x2, local copies, waits for them, and re-layouts  3.16 us

commit v1 on v0

--- a/solution.py
+++ b/solution.py
@@ -9,7 +9,6 @@
 from jax.experimental.pallas import tpu as pltpu
 from jax.sharding import PartitionSpec as P
 
-ITERS = 2
 CYCLES = 256
 MESH = pl.DeviceIdType.MESH
 F32 = jnp.float32
@@ -55,9 +54,9 @@
 
 def kernel(
     n, data, psf, cycles, cutoff, table, forward_z, inverse_z, out,
-    est, halo, corr_out, corr_in, corr_own, spread, gather, lat_f, lat_b,
-    dext, first, cs, onehot, spec, folded, red_out, red_in,
-    halo_send, halo_recv, corr_send, corr_recv, red_send, red_recv,
+    est, halo, corr_mine, corr_own, flat, both_out, both_in, last_out, last_in,
+    spread, gather, lat_f, lat_b, dext, first, cs, onehot, spec, red_out, red_in,
+    halo_send, halo_recv, both_send, both_recv, last_send, last_recv, red_send, red_recv,
 ):
     me = lax.axis_index("tile")
     has_left = me > 0
@@ -71,60 +70,69 @@
         return carry
 
     lax.fori_loop(1, n, greet, 0)
+
+    def neighbour(side):
+        return lax.rem(me + n - 1, n) if side == 0 else lax.rem(me + 1, n)
+
+    def halo_copy(h, side):
+        return pltpu.make_async_remote_copy(
+            src_ref=est.at[h, pl.ds(128 * side, 128)],
+            dst_ref=halo.at[h, 1 - side],
+            send_sem=halo_send.at[h, side],
+            recv_sem=halo_recv.at[h, 1 - side],
+            device_id={"tile": neighbour(side)},
+            device_id_type=MESH,
+        )
+
+    def both_copy(h, side):
+        return pltpu.make_async_remote_copy(
+            src_ref=both_out.at[h, side],
+            dst_ref=both_in.at[h, 1 - side],
+            send_sem=both_send.at[h, side],
+            recv_sem=both_recv.at[h, 1 - side],
+            device_id={"tile": neighbour(side)},
+            device_id_type=MESH,
+        )
+
+    def last_copy(h, side):
+        return pltpu.make_async_remote_copy(
+            src_ref=last_out.at[h, side],
+            dst_ref=last_in.at[h, 1 - side],
+            send_sem=last_send.at[h, side],
+            recv_sem=last_recv.at[h, 1 - side],
+            device_id={"tile": neighbour(side)},
+            device_id_type=MESH,
+        )
+
+    def on_side(side, action):
+        pl.when(has_left if side == 0 else has_right)(action)
+
+    def start(make, h):
+        for side in range(2):
+            on_side(side, lambda: make(h, side).start())
+
+    def wait_recv(make, h):
+        for side in range(2):
+            on_side(side, lambda: make(h, 1 - side).wait_recv())
+
+    def wait_send(make, h):
+        for side in range(2):
+            on_side(side, lambda: make(h, side).wait_send())
 
     for h in range(2):
         total = data[h, 0].astype(F32)
         for v in range(1, 4):
             total = total + data[h, v].astype(F32)
         est[h] = total * 0.25
-
-    pl.semaphore_wait(barrier, n - 1)
-
-    def halo_copy(it, h, side):
-        peer = lax.rem(me + n - 1, n) if side == 0 else lax.rem(me + 1, n)
-        return pltpu.make_async_remote_copy(
-            src_ref=est.at[h, pl.ds(128 * side, 128)],
-            dst_ref=halo.at[it, h, 1 - side],
-            send_sem=halo_send.at[it, h, side],
-            recv_sem=halo_recv.at[it, h, 1 - side],
-            device_id={"tile": peer},
-            device_id_type=MESH,
-        )
-
-    def corr_copy(it, h, side):
-        peer = lax.rem(me + n - 1, n) if side == 0 else lax.rem(me + 1, n)
-        return pltpu.make_async_remote_copy(
-            src_ref=corr_out.at[it, h, side],
-            dst_ref=corr_in.at[it, h, 1 - side],
-            send_sem=corr_send.at[it, h, side],
-            recv_sem=corr_recv.at[it, h, 1 - side],
-            device_id={"tile": peer},
-            device_id_type=MESH,
-        )
-
-    def on_side(side, action):
-        pl.when(has_left if side == 0 else has_right)(action)
-
-    def start(make, it, h):
-        for side in range(2):
-            on_side(side, lambda: make(it, h, side).start())
-
-    def wait_recv(make, it, h):
-        for side in range(2):
-            on_side(side, lambda: make(it, h, 1 - side).wait_recv())
-
-    def wait_send(make, it, h):
-        for side in range(2):
-            on_side(side, lambda: make(it, h, side).wait_send())
-
-    start(halo_copy, 0, 0)
-    start(halo_copy, 0, 1)
+        if h == 0:
+            pl.semaphore_wait(barrier, n - 1)
+        start(halo_copy, h)
 
     def clear(side):
-        for it in range(ITERS):
-            for h in range(2):
-                halo[it, h, side] = jnp.zeros((128, halo.shape[-1]), F32)
-                corr_in[it, h, side] = jnp.zeros((128, halo.shape[-1]), F32)
+        for h in range(2):
+            halo[h, side] = jnp.zeros(halo.shape[2:], F32)
+            both_in[h, side] = jnp.zeros(both_in.shape[2:], BF16)
+            last_in[h, side] = jnp.zeros(last_in.shape[2:], last_in.dtype)
 
     pl.when(jnp.logical_not(has_left))(lambda: clear(0))
     pl.when(jnp.logical_not(has_right))(lambda: clear(1))
@@ -137,7 +145,7 @@
     shift_x = col // depth - row // depth
 
     def taps_of(v, axis):
-        taps = [psf[v, axis, t] for t in range(9)]
+        taps = [psf[axis, v, t] for t in range(9)]
         total = taps[0]
         for t in range(1, 9):
             total = total + taps[t]
@@ -159,8 +167,11 @@
             band_z = select(shift_z, kz, 0, 9) * (nx * nz)
             at_v = pl.ds(pl.multiple_of(v * 128, 128), 128)
             for s in range(3):
-                low, high = split(select(shift_x + 4 * s, kx, max(4 * s - 3, 0), min(4 * s + 4, 9)) * band_z)
-                for part, value in enumerate((low, high, low)):
+                block = select(shift_x + 4 * s, kx, max(4 * s - 3, 0), min(4 * s + 4, 9)) * band_z
+                if mirrored:
+                    flat[s] += jnp.broadcast_to(jnp.sum(block, axis=1, keepdims=True), flat.shape[1:])
+                high, low = split(block)
+                for part, value in enumerate((high, low, high)):
                     if mirrored:
                         column = pl.ds(pl.multiple_of(v * 384 + part * 128, 128), 128)
                         gather[pl.ds(256 - 128 * s, 128), column] = value
@@ -168,8 +179,8 @@
                         spread[at_v, pl.ds(384 * s + 128 * part, 128)] = value
             lat = lat_b if mirrored else lat_f
             same = split(select(shift_y, ky, 0, 9) * ny)
-            after = split(select(shift_y + 128, ky, 0, 4 + 5) * ny)
-            before = split(select(shift_y - 128, ky, 0, 9) * ny)
+            after = split(select(shift_y + 128, ky, 5, 9) * ny)
+            before = split(select(shift_y - 128, ky, 0, 4) * ny)
             for part, which in enumerate((0, 1, 0)):
                 for b in range(2):
                     for i in range(3):
@@ -180,16 +191,14 @@
                             lat[v, b, pl.ds(384 * part + 128 * i, 128), pl.ds(128 * o, 128)] = value
         return carry
 
+    flat[...] = jnp.zeros_like(flat)
     lax.fori_loop(0, 4, build, 0)
 
-    bins = lax.broadcasted_iota(jnp.int32, (CYCLES, 256), 0)
-
-    def mark(k, carry):
-        ids = cycles[0, pl.ds(k, 1), pl.ds(0, 256)]
-        onehot[k] = jnp.where(bins == ids, 1.0, 0.0).astype(BF16)
-        return carry
-
-    lax.fori_loop(0, depth // 2 + 1, mark, 0)
+    ids = cycles[0, :, pl.ds(0, 256)].astype(F32)
+    ids = jnp.concatenate([ids, jnp.zeros((128 - depth, 256), F32)], axis=0).T
+    bins = lax.broadcasted_iota(jnp.int32, (256, CYCLES), 1).astype(F32)
+    for k in range(depth // 2 + 1):
+        onehot[pl.ds(256 * k, 256)] = jnp.where(bins == ids[:, k : k + 1], 1.0, 0.0).astype(BF16)
 
     def put_parts(ref, base, value):
         high, low = split(value)
@@ -204,16 +213,16 @@
             lhs = jnp.concatenate([high[:, at], high[:, at], low[:, at]], axis=1)
             yield dot(lhs, lat[v, b])
 
-    def sweep(it, h):
-        put_parts(dext, 0, halo[it, h, 0])
+    def sweep(h):
+        put_parts(dext, 0, halo[h, 0])
         put_parts(dext, 384, est[h, pl.ds(0, 128)])
         put_parts(dext, 768, est[h, pl.ds(128, 128)])
-        put_parts(dext, 1152, halo[it, h, 1])
+        put_parts(dext, 1152, halo[h, 1])
         for i in range(2):
             first[i] = dot(spread[...], dext[pl.ds(384 * i, 1152)])
 
-        def view(v, carry):
-            at_v = pl.ds(pl.multiple_of(v * 128, 128), 128)
+        for v in range(4):
+            at_v = pl.ds(v * 128, 128)
             value = jnp.concatenate([first[0, at_v], first[1, at_v]], axis=0)
             quotient = [
                 data[h, v, :, pl.ds(256 * b, 256)].astype(F32) / predicted
@@ -223,25 +232,57 @@
             for b, corrected in enumerate(along_y(quotient, lat_b, v)):
                 high, low = split(corrected)
                 for part, piece in enumerate((high, high, low)):
-                    at = pl.ds(pl.multiple_of(v * 384 + 128 * part, 128), 128)
+                    at = pl.ds(v * 384 + 128 * part, 128)
                     for side in range(2):
                         cs[side, at, pl.ds(256 * b, 256)] = piece[128 * side : 128 * side + 128]
-            return carry
-
-        lax.fori_loop(0, 4, view, 0)
+
         r0 = dot(gather[...], cs[0])
-        corr_out[it, h, 0] = r0[:128]
+        corr_mine[h, 0] = r0[:128]
         corr_own[h] = r0[128:]
         r1 = dot(gather[...], cs[1])
-        corr_out[it, h, 1] = r1[256:]
+        corr_mine[h, 1] = r1[256:]
         corr_own[h] += r1[:256]
 
-    def update(it, h):
-        wait_send(halo_copy, it, h)
-        wait_recv(corr_copy, it, h)
-        for side in range(2):
-            at = pl.ds(128 * side, 128)
-            est[h, at] = est[h, at] * (0.25 * (corr_own[h, at] + corr_in[it, h, side]))
+    def wide(value):
+        return jnp.concatenate([value] * (halo.shape[-1] // 128), axis=1)
+
+    def flat_part(side):
+        return wide(flat[0] if side == 0 else flat[2])
+
+    def flat_own(side):
+        return wide(flat[1] + (flat[2] if side == 0 else flat[0]))
+
+    def send_both(h):
+        for side in range(2):
+            both_out[h, side, pl.ds(0, 128)] = (corr_mine[h, side] - flat_part(1 - side)).astype(BF16)
+            both_out[h, side, pl.ds(128, 128)] = (
+                corr_own[h, pl.ds(128 * side, 128)] - flat_own(side)
+            ).astype(BF16)
+        start(both_copy, h)
+
+    def send_last(h):
+        for side in range(2):
+            last_out[h, side] = (corr_mine[h, side] - flat_part(1 - side)).astype(last_out.dtype)
+        start(last_copy, h)
+
+    def scale_own(h, side, received):
+        at = pl.ds(128 * side, 128)
+        near = has_left if side == 0 else has_right
+        outside = jnp.where(near, flat_part(side) + received.astype(F32), 0.0)
+        est[h, at] = est[h, at] * (0.25 * (corr_own[h, at] + outside))
+
+    def update_both(h):
+        wait_send(halo_copy, h)
+        wait_recv(both_copy, h)
+        for side in range(2):
+            scale_own(h, side, both_in[h, side, pl.ds(0, 128)])
+            theirs = flat_own(1 - side) + both_in[h, side, pl.ds(128, 128)].astype(F32)
+            halo[h, side] = halo[h, side] * (0.25 * (corr_mine[h, side] + theirs))
+
+    def update_last(h):
+        wait_recv(last_copy, h)
+        for side in range(2):
+            scale_own(h, side, last_in[h, side])
 
     def spectrum(h):
         rows = dot(est[h].astype(BF16), table[...])
@@ -252,17 +293,17 @@
             high, low = split(both)
             spec[h, g] = dot(forward_z[...], jnp.concatenate([high, high, low], axis=0))
 
-    for it in range(ITERS):
-        for h in range(2):
-            wait_recv(halo_copy, it, h)
-            sweep(it, h)
-            start(corr_copy, it, h)
-        for h in range(2):
-            update(it, h)
-            if it + 1 < ITERS:
-                start(halo_copy, it + 1, h)
-            else:
-                spectrum(h)
+    for h in range(2):
+        wait_recv(halo_copy, h)
+        sweep(h)
+        send_both(h)
+    for h in range(2):
+        update_both(h)
+        sweep(h)
+        send_last(h)
+    for h in range(2):
+        update_last(h)
+        spectrum(h)
 
     lateral = data.shape[3]
     half = depth // 2
@@ -277,8 +318,8 @@
     lane = lax.broadcasted_iota(jnp.int32, (1, 256), 1)
     weight_l = jnp.where(lane == 0, 1.0, 2.0)
     rows16 = lax.broadcasted_iota(jnp.int32, (half, 256), 0)
-    folded[...] = jnp.zeros_like(folded)
     edge = []
+    cells = []
     for q, (a, b) in enumerate(((0, 1), (0, 0), (1, 1))):
         total = power(a, b)
         edge.append(jnp.sum(total[:, 256:257], axis=0, keepdims=True))
@@ -286,20 +327,15 @@
         high = total[half:, :256]
         pairs = (low + jnp.where(rows16 == 0, 0.0, high)) * weight_l
         last = high[:1] * weight_l
-        for k in range(half):
-            folded[k, q : q + 1] = pairs[k : k + 1]
-        folded[half, q : q + 1] = last
-
-    binned = jnp.zeros((32, CYCLES), F32)
+        cells.append([pairs[k : k + 1] for k in range(half)] + [high[:1] * weight_l])
+
+    terms = []
     for k in range(half + 1):
-        value = folded[k]
+        value = jnp.concatenate([cells[q][k] for q in range(3)] + [jnp.zeros((5, 256), F32)], axis=0)
         a = value.astype(BF16).astype(F32)
         b = (value - a).astype(BF16).astype(F32)
-        c = value - a - b
-        lhs = jnp.concatenate([a, b, c, jnp.zeros_like(a)], axis=0).astype(BF16)
-        binned = binned + lax.dot_general(
-            lhs, onehot[k], (((1,), (1,)), ((), ())), preferred_element_type=F32
-        )
+        terms.append(jnp.concatenate([a, b, value - a - b, jnp.zeros_like(a)], axis=0).astype(BF16))
+    binned = dot(jnp.concatenate(terms, axis=1), onehot[...])
     binned = binned[0:8] + binned[8:16] + binned[16:24]
     bin_row = lax.broadcasted_iota(jnp.int32, (8, CYCLES), 0)
     bin_lane = lax.broadcasted_iota(jnp.int32, (8, CYCLES), 1)
@@ -365,9 +401,9 @@
             inner[128:], table[:, pl.ds(lateral, lateral)]
         )
 
-    for it in range(ITERS):
-        for h in range(2):
-            wait_send(corr_copy, it, h)
+    for h in range(2):
+        wait_send(both_copy, h)
+        wait_send(last_copy, h)
 
 
 def body(data_halves, psf_taps, cycle_map, cutoff):
@@ -385,10 +421,14 @@
         out_specs=vmem,
         scratch_shapes=[
             pltpu.VMEM((2, rows, lateral), F32),
-            pltpu.VMEM((ITERS, 2, 2, 128, lateral), F32),
-            pltpu.VMEM((ITERS, 2, 2, 128, lateral), F32),
-            pltpu.VMEM((ITERS, 2, 2, 128, lateral), F32),
+            pltpu.VMEM((2, 2, 128, lateral), F32),
+            pltpu.VMEM((2, 2, 128, lateral), F32),
             pltpu.VMEM((2, rows, lateral), F32),
+            pltpu.VMEM((3, 128, 128), F32),
+            pltpu.VMEM((2, 2, 256, lateral), BF16),
+            pltpu.VMEM((2, 2, 256, lateral), BF16),
+            pltpu.VMEM((2, 2, 128, lateral), BF16),
+            pltpu.VMEM((2, 2, 128, lateral), BF16),
             pltpu.VMEM((512, 1152), BF16),
             pltpu.VMEM((384, 1536), BF16),
             pltpu.VMEM((4, 2, 1152, 256), BF16),
@@ -396,15 +436,16 @@
             pltpu.VMEM((1536, lateral), BF16),
             pltpu.VMEM((2, 512, lateral), F32),
             pltpu.VMEM((2, 1536, lateral), BF16),
-            pltpu.VMEM((depth // 2 + 1, CYCLES, 256), BF16),
+            pltpu.VMEM(((depth // 2 + 1) * 256, CYCLES), BF16),
             pltpu.VMEM((2, 2, rows, lateral), F32),
-            pltpu.VMEM((depth // 2 + 1, 8, 256), F32),
             pltpu.VMEM((8, CYCLES), F32),
             pltpu.VMEM((n, 8, CYCLES), F32),
-            dma((ITERS, 2, 2)),
-            dma((ITERS, 2, 2)),
-            dma((ITERS, 2, 2)),
-            dma((ITERS, 2, 2)),
+            dma((2, 2)),
+            dma((2, 2)),
+            dma((2, 2)),
+            dma((2, 2)),
+            dma((2, 2)),
+            dma((2, 2)),
             dma((n,)),
             dma((n,)),
         ],
@@ -413,7 +454,7 @@
         ),
     )(
         data_halves.reshape(halves, views, rows, lateral),
-        psf_taps,
+        jnp.transpose(psf_taps, (1, 0, 2)),
         cycle_map,
         cutoff,
         jnp.asarray(table),

time: 75.8 us -> 58 us (0.77)
  Pallas kernels: 71.7 us -> 55.3 us
  local copies, waits for them, and re-layouts: 3.16 us -> 1.87 us
    pallas_call x1, Pallas kernels: 71.7 us -> 55.3 us  [body(): pl.pallas_call(functools.partial(kernel, n), out_shape=jax.ShapeDtypeStru...]
    unnamed x2 -> x1, local copies, waits for them, and re-layouts: 3.16 us -> 1.87 us
where the time goes in v1:
time: 58 us; the launch traced here: 57.8 us
  Pallas kernels  55.3 us (95%)
  local copies, waits for them, and re-layouts  1.87 us (3%)
  between operations  0.66 us (1%)
    pallas_call x1, Pallas kernels, body(): pl.pallas_call(functools.partial(kernel, n), out_shape=jax.ShapeDtypeStru...  55.3 us
    unnamed x1, local copies, waits for them, and re-layouts  1.87 us

profile of v1, /device:TPU:0, one launch (start us, length us, event | category | flops | bytes accessed | tf_op | source)
XLA Modules:
  0.0 57.8 jit_solution(3320475069800170494)
XLA Ops:
  0.7 55.3 %shard_map.73 = f32[256,512]{1,0:T(8,128)} custom-call(bf16[2,4,256,512]{3,2,1,0:T(8,128)(2,1)} %bitcast.3, f32[3,4,9]{2,1,0:T(4,128)} %bitcast.5, s32[1,32,512]{2,1,0:T(8,128)} %cycles.1, s32[1]{0:T(128)S(6)} %copy.9.cutoff, bf16[512,1024]{1,0:T(8,128)(2,1)} %constant.6.clone.table, bf16[256,768]{1,0:T(8,128)(2,1)} %constant.7.clone.forward_z, ...), custom_call_target="tpu_custom_call" | custom-call | tf_op jit(solution)/shard_map/pallas_call | solution.py:417
  55.9 1.9 %copy.10 = f32[8,32,512]{2,1,0:T(8,128)} copy(f32[8,32,512]{2,1,0:T(8,128)} %bitcast.4) | data formatting | bytes 1048576

commit v2 on v1

--- a/solution.py
+++ b/solution.py
@@ -53,7 +53,8 @@
 
 
 def kernel(
-    n, data, psf, cycles, cutoff, table, forward_z, inverse_z, out,
+    n, data_far, psf, cycles, cutoff, table_far, forward_far, inverse_far, out,
+    data, table, forward_z, inverse_z, near_sem,
     est, halo, corr_mine, corr_own, flat, both_out, both_in, last_out, last_in,
     spread, gather, lat_f, lat_b, dext, first, cs, onehot, spec, red_out, red_in,
     halo_send, halo_recv, both_send, both_recv, last_send, last_recv, red_send, red_recv,
@@ -61,6 +62,14 @@
     me = lax.axis_index("tile")
     has_left = me > 0
     has_right = me < n - 1
+
+    near = [pltpu.make_async_copy(data_far.at[h], data.at[h], near_sem.at[h]) for h in range(2)]
+    near += [
+        pltpu.make_async_copy(far, to, near_sem.at[i])
+        for i, far, to in ((2, table_far, table), (3, forward_far, forward_z), (4, inverse_far, inverse_z))
+    ]
+    for copy in near:
+        copy.start()
 
     barrier = pltpu.get_barrier_semaphore()
 
@@ -120,6 +129,7 @@
             on_side(side, lambda: make(h, side).wait_send())
 
     for h in range(2):
+        near[h].wait()
         total = data[h, 0].astype(F32)
         for v in range(1, 4):
             total = total + data[h, v].astype(F32)
@@ -213,7 +223,7 @@
             lhs = jnp.concatenate([high[:, at], high[:, at], low[:, at]], axis=1)
             yield dot(lhs, lat[v, b])
 
-    def sweep(h):
+    def sweep(h, send):
         put_parts(dext, 0, halo[h, 0])
         put_parts(dext, 384, est[h, pl.ds(0, 128)])
         put_parts(dext, 768, est[h, pl.ds(128, 128)])
@@ -221,14 +231,21 @@
         for i in range(2):
             first[i] = dot(spread[...], dext[pl.ds(384 * i, 1152)])
 
-        for v in range(4):
+        def predict(v):
             at_v = pl.ds(v * 128, 128)
             value = jnp.concatenate([first[0, at_v], first[1, at_v]], axis=0)
-            quotient = [
-                data[h, v, :, pl.ds(256 * b, 256)].astype(F32) / predicted
-                for b, predicted in enumerate(along_y(value, lat_f, v))
-            ]
-            quotient = jnp.concatenate(quotient, axis=1)
+            return list(along_y(value, lat_f, v))
+
+        def divide(v, predicted):
+            quotient = []
+            for b in range(2):
+                seen = data[h, v, :, pl.ds(256 * b, 256)].astype(F32)
+                inverse = pl.reciprocal(predicted[b], approx=True)
+                value = seen * inverse
+                quotient.append(value + inverse * (seen - predicted[b] * value))
+            return jnp.concatenate(quotient, axis=1)
+
+        def spread_back(v, quotient):
             for b, corrected in enumerate(along_y(quotient, lat_b, v)):
                 high, low = split(corrected)
                 for part, piece in enumerate((high, high, low)):
@@ -236,6 +253,15 @@
                     for side in range(2):
                         cs[side, at, pl.ds(256 * b, 256)] = piece[128 * side : 128 * side + 128]
 
+        predicted = predict(0)
+        for v in range(4):
+            following = predict(v + 1) if v < 3 else None
+            spread_back(v, divide(v, predicted))
+            predicted = following
+
+        send(h)
+
+    def gather_both(h):
         r0 = dot(gather[...], cs[0])
         corr_mine[h, 0] = r0[:128]
         corr_own[h] = r0[128:]
@@ -253,6 +279,7 @@
         return wide(flat[1] + (flat[2] if side == 0 else flat[0]))
 
     def send_both(h):
+        gather_both(h)
         for side in range(2):
             both_out[h, side, pl.ds(0, 128)] = (corr_mine[h, side] - flat_part(1 - side)).astype(BF16)
             both_out[h, side, pl.ds(128, 128)] = (
@@ -262,8 +289,11 @@
 
     def send_last(h):
         for side in range(2):
-            last_out[h, side] = (corr_mine[h, side] - flat_part(1 - side)).astype(last_out.dtype)
+            part = dot(gather[pl.ds(256 * side, 128)], cs[side])
+            last_out[h, side] = (part - flat_part(1 - side)).astype(last_out.dtype)
         start(last_copy, h)
+        corr_own[h] = dot(gather[pl.ds(128, 256)], cs[0])
+        corr_own[h] += dot(gather[pl.ds(0, 256)], cs[1])
 
     def scale_own(h, side, received):
         at = pl.ds(128 * side, 128)
@@ -295,15 +325,10 @@
 
     for h in range(2):
         wait_recv(halo_copy, h)
-        sweep(h)
-        send_both(h)
+        sweep(h, send_both)
     for h in range(2):
         update_both(h)
-        sweep(h)
-        send_last(h)
-    for h in range(2):
-        update_last(h)
-        spectrum(h)
+        sweep(h, send_last)
 
     lateral = data.shape[3]
     half = depth // 2
@@ -315,13 +340,21 @@
                 total = total + spec[a, g, pl.ds(at, depth)] * spec[b, g, pl.ds(at, depth)]
         return total
 
+    for copy in near[2:]:
+        copy.wait()
+    update_last(0)
+    spectrum(0)
+    power_0 = power(0, 0)
+    update_last(1)
+    spectrum(1)
+    powers = (power(0, 1), power_0, power(1, 1))
+
     lane = lax.broadcasted_iota(jnp.int32, (1, 256), 1)
     weight_l = jnp.where(lane == 0, 1.0, 2.0)
     rows16 = lax.broadcasted_iota(jnp.int32, (half, 256), 0)
     edge = []
     cells = []
-    for q, (a, b) in enumerate(((0, 1), (0, 0), (1, 1))):
-        total = power(a, b)
+    for q, total in enumerate(powers):
         edge.append(jnp.sum(total[:, 256:257], axis=0, keepdims=True))
         low = total[:half, :256]
         high = total[half:, :256]
@@ -413,13 +446,19 @@
     table, forward_z, inverse_z = constants(depth, lateral)
     vmem = pl.BlockSpec(memory_space=pltpu.VMEM)
     smem = pl.BlockSpec(memory_space=pltpu.SMEM)
+    far = pl.BlockSpec(memory_space=pl.ANY)
     dma = pltpu.SemaphoreType.DMA
     joined = pl.pallas_call(
         functools.partial(kernel, n),
         out_shape=jax.ShapeDtypeStruct((rows, lateral), F32),
-        in_specs=[vmem, smem, vmem, smem, vmem, vmem, vmem],
+        in_specs=[far, smem, vmem, smem, far, far, far],
         out_specs=vmem,
         scratch_shapes=[
+            pltpu.VMEM((halves, views, rows, lateral), BF16),
+            pltpu.VMEM(table.shape, BF16),
+            pltpu.VMEM(forward_z.shape, BF16),
+            pltpu.VMEM(inverse_z.shape, BF16),
+            dma((5,)),
             pltpu.VMEM((2, rows, lateral), F32),
             pltpu.VMEM((2, 2, 128, lateral), F32),
             pltpu.VMEM((2, 2, 128, lateral), F32),

time: 58 us -> 55.5 us (0.957)
  Pallas kernels: 55.3 us -> 52.8 us
    pallas_call x1, Pallas kernels: 55.3 us -> 52.8 us  [body(): pl.pallas_call(functools.partial(kernel, n), out_shape=jax.ShapeDtypeStru...]
where the time goes in v2:
time: 55.5 us; the launch traced here: 55.3 us
  Pallas kernels  52.8 us (95%)
  local copies, waits for them, and re-layouts  1.87 us (3%)
  between operations  0.66 us (1%)
    pallas_call x1, Pallas kernels, body(): pl.pallas_call(functools.partial(kernel, n), out_shape=jax.ShapeDtypeStru...  52.8 us
    unnamed x1, local copies, waits for them, and re-layouts  1.87 us

profile of v2, /device:TPU:0, one launch (start us, length us, event | category | flops | bytes accessed | tf_op | source)
XLA Modules:
  0.0 55.3 jit_solution(4800083215834401108)
XLA Ops:
  0.7 52.8 %shard_map.73 = f32[256,512]{1,0:T(8,128)} custom-call(bf16[2,4,256,512]{3,2,1,0:T(8,128)(2,1)} %bitcast.3, f32[3,4,9]{2,1,0:T(4,128)} %bitcast.5, s32[1,32,512]{2,1,0:T(8,128)} %cycles.1, s32[1]{0:T(128)S(6)} %copy.9.cutoff, bf16[512,1024]{1,0:T(8,128)(2,1)} %constant.6.clone.table_far, bf16[256,768]{1,0:T(8,128)(2,1)} %constant.7.clone.forward_far, ...), custom_call_target="tpu_custom_call" | custom-call | tf_op jit(solution)/shard_map/pallas_call | solution.py:451
  53.4 1.9 %copy.10 = f32[8,32,512]{2,1,0:T(8,128)} copy(f32[8,32,512]{2,1,0:T(8,128)} %bitcast.4) | data formatting | bytes 1048576

commit v3 on v2

--- a/solution.py
+++ b/solution.py
@@ -192,13 +192,12 @@
             after = split(select(shift_y + 128, ky, 5, 9) * ny)
             before = split(select(shift_y - 128, ky, 0, 4) * ny)
             for part, which in enumerate((0, 1, 0)):
-                for b in range(2):
-                    for i in range(3):
-                        for o in range(2):
-                            step = (i + b) - (o + 2 * b)
-                            value = {0: same, 1: after, -1: before}.get(step)
-                            value = zero if value is None else value[which]
-                            lat[v, b, pl.ds(384 * part + 128 * i, 128), pl.ds(128 * o, 128)] = value
+                for i in range(2):
+                    for o in range(2):
+                        at = pl.ds(256 * part + 128 * i, 128), pl.ds(128 * o, 128)
+                        value = (same, after, before)[i - o][which]
+                        lat[(v, 0) + at] = value
+                        lat[(v, 1) + at] = zero if i == o else value
         return carry
 
     flat[...] = jnp.zeros_like(flat)
@@ -216,12 +215,17 @@
         ref[pl.ds(base + 128, 128)] = high
         ref[pl.ds(base + 256, 128)] = low
 
+    def three(high, low, at):
+        return jnp.concatenate([high[:, at], high[:, at], low[:, at]], axis=1)
+
     def along_y(value, lat, v):
         high, low = split(value)
-        for b in range(2):
-            at = slice(128 * b, 128 * b + 384)
-            lhs = jnp.concatenate([high[:, at], high[:, at], low[:, at]], axis=1)
-            yield dot(lhs, lat[v, b])
+        halves = [three(high, low, slice(0, 256)), three(high, low, slice(256, 512))]
+        inside = dot(jnp.concatenate(halves, axis=0), lat[v, 0])
+        across = dot(three(high, low, slice(128, 384)), lat[v, 1])
+        rows = value.shape[0]
+        yield jnp.concatenate([inside[:rows, :128], inside[:rows, 128:] + across[:, :128]], axis=1)
+        yield jnp.concatenate([inside[rows:, :128] + across[:, 128:], inside[rows:, 128:]], axis=1)
 
     def sweep(h, send):
         put_parts(dext, 0, halo[h, 0])
@@ -470,8 +474,8 @@
             pltpu.VMEM((2, 2, 128, lateral), BF16),
             pltpu.VMEM((512, 1152), BF16),
             pltpu.VMEM((384, 1536), BF16),
-            pltpu.VMEM((4, 2, 1152, 256), BF16),
-            pltpu.VMEM((4, 2, 1152, 256), BF16),
+            pltpu.VMEM((4, 2, 768, 256), BF16),
+            pltpu.VMEM((4, 2, 768, 256), BF16),
             pltpu.VMEM((1536, lateral), BF16),
             pltpu.VMEM((2, 512, lateral), F32),
             pltpu.VMEM((2, 1536, lateral), BF16),

time: 55.5 us -> 54.4 us (0.980)
  Pallas kernels: 52.8 us -> 51.7 us
    pallas_call x1, Pallas kernels: 52.8 us -> 51.7 us  [body(): pl.pallas_call(functools.partial(kernel, n), out_shape=jax.ShapeDtypeStru...]
where the time goes in v3:
time: 54.4 us; the launch traced here: 54.2 us
  Pallas kernels  51.7 us (95%)
  local copies, waits for them, and re-layouts  1.87 us (3%)
  between operations  0.66 us (1%)
    pallas_call x1, Pallas kernels, body(): pl.pallas_call(functools.partial(kernel, n), out_shape=jax.ShapeDtypeStru...  51.7 us
    unnamed x1, local copies, waits for them, and re-layouts  1.87 us

profile of v3, /device:TPU:0, one launch (start us, length us, event | category | flops | bytes accessed | tf_op | source)
XLA Modules:
  0.0 54.2 jit_solution(10971363381006028100)
XLA Ops:
  0.7 51.7 %shard_map.73 = f32[256,512]{1,0:T(8,128)} custom-call(bf16[2,4,256,512]{3,2,1,0:T(8,128)(2,1)} %bitcast.3, f32[3,4,9]{2,1,0:T(4,128)} %bitcast.5, s32[1,32,512]{2,1,0:T(8,128)} %cycles.1, s32[1]{0:T(128)S(6)} %copy.9.cutoff, bf16[512,1024]{1,0:T(8,128)(2,1)} %constant.6.clone.table_far, bf16[256,768]{1,0:T(8,128)(2,1)} %constant.7.clone.forward_far, ...), custom_call_target="tpu_custom_call" | custom-call | tf_op jit(solution)/shard_map/pallas_call | solution.py:455
  52.4 1.9 %copy.10 = f32[8,32,512]{2,1,0:T(8,128)} copy(f32[8,32,512]{2,1,0:T(8,128)} %bitcast.4) | data formatting | bytes 1048576

commit v4 on v3

--- a/solution.py
+++ b/solution.py
@@ -203,12 +203,6 @@
     flat[...] = jnp.zeros_like(flat)
     lax.fori_loop(0, 4, build, 0)
 
-    ids = cycles[0, :, pl.ds(0, 256)].astype(F32)
-    ids = jnp.concatenate([ids, jnp.zeros((128 - depth, 256), F32)], axis=0).T
-    bins = lax.broadcasted_iota(jnp.int32, (256, CYCLES), 1).astype(F32)
-    for k in range(depth // 2 + 1):
-        onehot[pl.ds(256 * k, 256)] = jnp.where(bins == ids[:, k : k + 1], 1.0, 0.0).astype(BF16)
-
     def put_parts(ref, base, value):
         high, low = split(value)
         ref[pl.ds(base, 128)] = high
@@ -227,14 +221,30 @@
         yield jnp.concatenate([inside[:rows, :128], inside[:rows, 128:] + across[:, :128]], axis=1)
         yield jnp.concatenate([inside[rows:, :128] + across[:, 128:], inside[rows:, 128:]], axis=1)
 
-    def sweep(h, send):
-        put_parts(dext, 0, halo[h, 0])
+    def put_own(h):
         put_parts(dext, 384, est[h, pl.ds(0, 128)])
         put_parts(dext, 768, est[h, pl.ds(128, 128)])
+
+    def put_halo(h):
+        put_parts(dext, 0, halo[h, 0])
         put_parts(dext, 1152, halo[h, 1])
+
+    def blur_all(h):
+        put_own(h)
+        put_halo(h)
         for i in range(2):
             first[i] = dot(spread[...], dext[pl.ds(384 * i, 1152)])
 
+    def blur_early(h):
+        put_own(h)
+        for i in range(2):
+            first[i] = dot(spread[:, pl.ds(384 - 384 * i, 768)], dext[pl.ds(384, 768)])
+        wait_recv(halo_copy, h)
+        put_halo(h)
+        for i in range(2):
+            first[i] += dot(spread[:, pl.ds(768 * i, 384)], dext[pl.ds(1152 * i, 384)])
+
+    def sweep(h, send):
         def predict(v):
             at_v = pl.ds(v * 128, 128)
             value = jnp.concatenate([first[0, at_v], first[1, at_v]], axis=0)
@@ -328,10 +338,15 @@
             spec[h, g] = dot(forward_z[...], jnp.concatenate([high, high, low], axis=0))
 
     for h in range(2):
-        wait_recv(halo_copy, h)
+        if h == 0:
+            blur_early(h)
+        else:
+            wait_recv(halo_copy, h)
+            blur_all(h)
         sweep(h, send_both)
     for h in range(2):
         update_both(h)
+        blur_all(h)
         sweep(h, send_last)
 
     lateral = data.shape[3]
@@ -349,6 +364,13 @@
     update_last(0)
     spectrum(0)
     power_0 = power(0, 0)
+
+    ids = cycles[0, :, pl.ds(0, 256)].astype(F32)
+    ids = jnp.concatenate([ids, jnp.zeros((128 - depth, 256), F32)], axis=0).T
+    bins = lax.broadcasted_iota(jnp.int32, (256, CYCLES), 1).astype(F32)
+    for k in range(depth // 2 + 1):
+        onehot[pl.ds(256 * k, 256)] = jnp.where(bins == ids[:, k : k + 1], 1.0, 0.0).astype(BF16)
+
     update_last(1)
     spectrum(1)
     powers = (power(0, 1), power_0, power(1, 1))

time: 54.4 us -> 53.3 us (0.980)
  Pallas kernels: 51.7 us -> 50.6 us
    pallas_call x1, Pallas kernels: 51.7 us -> 50.6 us  [body(): pl.pallas_call(functools.partial(kernel, n), out_shape=jax.ShapeDtypeStru...]
where the time goes in v4:
time: 53.3 us; the launch traced here: 53.1 us
  Pallas kernels  50.6 us (95%)
  local copies, waits for them, and re-layouts  1.87 us (4%)
  between operations  0.66 us (1%)
    pallas_call x1, Pallas kernels, body(): pl.pallas_call(functools.partial(kernel, n), out_shape=jax.ShapeDtypeStru...  50.6 us
    unnamed x1, local copies, waits for them, and re-layouts  1.87 us

profile of v4, /device:TPU:0, one launch (start us, length us, event | category | flops | bytes accessed | tf_op | source)
XLA Modules:
  0.0 53.1 jit_solution(11207538320539045785)
XLA Ops:
  0.7 50.6 %shard_map.73 = f32[256,512]{1,0:T(8,128)} custom-call(bf16[2,4,256,512]{3,2,1,0:T(8,128)(2,1)} %bitcast.3, f32[3,4,9]{2,1,0:T(4,128)} %bitcast.5, s32[1,32,512]{2,1,0:T(8,128)} %cycles.1, s32[1]{0:T(128)S(6)} %copy.9.cutoff, bf16[512,1024]{1,0:T(8,128)(2,1)} %constant.6.clone.table_far, bf16[256,768]{1,0:T(8,128)(2,1)} %constant.7.clone.forward_far, ...), custom_call_target="tpu_custom_call" | custom-call | tf_op jit(solution)/shard_map/pallas_call | solution.py:477
  51.3 1.9 %copy.10 = f32[8,32,512]{2,1,0:T(8,128)} copy(f32[8,32,512]{2,1,0:T(8,128)} %bitcast.4) | data formatting | bytes 1048576
